TPU v7x, 32 devices: a whole 2x2x4 slice. The times are simulated.
32 devices in a mesh: tm: 8 (over y, x, core), patch: 4 (over z).
Axes of the slice: x: 2, y: 2, z: 4, core: 2. Of those that a mesh axis runs over, the one named last changes fastest.
Arguments:
- frames_in: bfloat16 [64, 256, 1024], P('tm', 'patch'), may hold values from -6 to 6
- codes: int32 [64, 256], P('tm', 'patch'), may hold values from 0 to 1023
- gain_space: float32 [1024], replicated, may hold values from 0.1 to 1.9
- qkv_space: bfloat16 [1024, 3072], replicated, may hold values from -0.1875 to 0.1875
- out_space: bfloat16 [1024, 1024], replicated, may hold values from -0.75 to 0.75
- scale_space: float32 [16], replicated, may hold values from 3 to 12
- gain_time: float32 [1024], replicated, may hold values from 0.1 to 1.9
- qkv_time: bfloat16 [1024, 3072], replicated, may hold values from -0.1875 to 0.1875
- out_time: bfloat16 [1024, 1024], replicated, may hold values from -0.75 to 0.75
- scale_time: float32 [16], replicated, may hold values from 3 to 12
- codebook: bfloat16 [1024, 1024], replicated, may hold values from -6 to 6
Outputs:
- encoded: bfloat16 [64, 256, 1024], P('tm', 'patch')
- commitment: bfloat16 [64, 256, 1024], P('tm', 'patch')
All inputs are finite; a program needn't handle non-finite values.
Results may differ from a plain program's by a relative error of at most 0.02.
Values may be sent and summed in bfloat16 or wider, within the bound.
A program may use at most 192 MiB of HBM per device.

v0:
```python
import jax
import jax.numpy as jnp
from jax import lax
from jax.sharding import PartitionSpec as P

H = 16
HD = 64


def norm_rows(stream, gain):
    wide = stream.astype(jnp.float32)
    return (wide * lax.rsqrt(jnp.mean(wide * wide, -1, keepdims=True) + 1e-05) * gain).astype(
        jnp.bfloat16
    )


def project(stream, gain, weights, scale):
    width = stream.shape[-1]
    head_size = width // H
    normed = norm_rows(stream, gain)
    lead = normed.shape[:-1]
    qkv = jnp.dot(normed.reshape(-1, width), weights, preferred_element_type=jnp.float32)
    query = qkv[:, :width].reshape(-1, H, head_size)
    key = qkv[:, width : 2 * width].reshape(-1, H, head_size)
    value = qkv[:, 2 * width :]
    query = (
        query
        * lax.rsqrt(jnp.mean(query * query, -1, keepdims=True) + 1e-06)
        * (scale[:, None] / head_size)
    )
    key = key * lax.rsqrt(jnp.mean(key * key, -1, keepdims=True) + 1e-06)
    return (
        query.reshape(lead + (width,)).astype(jnp.bfloat16),
        key.reshape(lead + (width,)).astype(jnp.bfloat16),
        value.reshape(lead + (width,)).astype(jnp.bfloat16),
    )


def group_lanes(array):
    batch, count, width = array.shape
    lanes = 128
    return jnp.transpose(array.reshape(batch, count, width // lanes, lanes), (0, 2, 1, 3))


def merge_lanes(array):
    batch, groups, count, lanes = array.shape
    return jnp.transpose(array, (0, 2, 1, 3)).reshape(batch, count, groups * lanes)


def head_terms(query, key, value, allowed):
    lanes = query.shape[-1]
    heads = lanes // HD
    lane_head = jnp.arange(lanes, dtype=jnp.int32) // HD
    out_shape = query.shape[:3] + (lanes,)
    total = jnp.zeros(out_shape, jnp.float32)
    denom = jnp.ones(out_shape, jnp.float32)
    for head in range(heads):
        picked = lane_head == head
        masked = jnp.where(picked, query, jnp.zeros_like(query))
        scores = jnp.einsum("bjnc,bjmc->bjnm", masked, key, preferred_element_type=jnp.float32)
        weight = jnp.exp(scores)
        if allowed is not None:
            weight = jnp.where(allowed, weight, 0.0)
        weight = weight.astype(jnp.bfloat16)
        part = jnp.einsum("bjnm,bjmc->bjnc", weight, value, preferred_element_type=jnp.float32)
        total = jnp.where(picked, part, total)
        denom = jnp.where(picked, jnp.sum(weight.astype(jnp.float32), -1)[..., None], denom)
    return (total, denom)


def shards(
    frames_in,
    codes,
    gain_space,
    qkv_space,
    out_space,
    scale_space,
    gain_time,
    qkv_time,
    out_time,
    scale_time,
    codebook,
):
    f_local, p_local, width = frames_in.shape
    own = lax.all_to_all(frames_in, "patch", split_axis=0, concat_axis=1, tiled=True)
    query, key, value = project(own, gain_space, qkv_space, scale_space)
    total, denom = head_terms(group_lanes(query), group_lanes(key), group_lanes(value), None)
    attn_s = merge_lanes(total / denom).astype(jnp.bfloat16)
    stream = own.astype(jnp.float32) + jnp.dot(
        attn_s.reshape(-1, width), out_space, preferred_element_type=jnp.float32
    ).reshape(own.shape)
    stream = stream.astype(jnp.bfloat16)
    stream = lax.all_to_all(stream, "patch", split_axis=1, concat_axis=0, tiled=True)
    stream = lax.all_to_all(stream, "tm", split_axis=1, concat_axis=0, tiled=True)
    stream = jnp.transpose(stream, (1, 0, 2))
    query, key, value = project(stream, gain_time, qkv_time, scale_time)
    order = jnp.arange(stream.shape[1], dtype=jnp.int32)
    allowed = order[:, None] >= order[None, :]
    part, part_denom = head_terms(
        group_lanes(query), group_lanes(key), group_lanes(value), allowed
    )
    attn_t = merge_lanes(part / part_denom).reshape(-1, width).astype(jnp.bfloat16)
    output = stream.astype(jnp.float32) + jnp.dot(
        attn_t, out_time, preferred_element_type=jnp.float32
    ).reshape(stream.shape)
    output = jnp.transpose(output.astype(jnp.bfloat16), (1, 0, 2))
    output = lax.all_to_all(output, "tm", split_axis=0, concat_axis=1, tiled=True)
    code_count = codebook.shape[0]
    one_hot = (codes[..., None] == jnp.arange(code_count, dtype=jnp.int32)).astype(jnp.bfloat16)
    chosen = jnp.dot(
        one_hot.reshape(-1, code_count), codebook, preferred_element_type=jnp.float32
    ).reshape(f_local, p_local, width)
    return (output, (output.astype(jnp.float32) - chosen).astype(jnp.bfloat16))


def solution(mesh):
    return jax.shard_map(
        shards,
        mesh=mesh,
        in_specs=(
            P("tm", "patch", None),
            P("tm", "patch"),
            P(),
            P(),
            P(),
            P(),
            P(),
            P(),
            P(),
            P(),
            P(),
        ),
        out_specs=(P("tm", "patch", None), P("tm", "patch", None)),
        check_vma=False,
    )
```

profile of v0, /device:TPU:1, one launch (start us, length us, event | category | flops | bytes accessed | tf_op | source)
XLA Modules:
  0.0 217.2 jit_solution(5615896388850048)
XLA Ops:
  0.7 5.6 %all-to-all-start = ((bf16[8,64,1024]{2,1,0:T(8,128)(2,1)}), bf16[8,64,1024]{2,1,0:T(8,128)(2,1)S(1)}, u32[]{:S(2)}, u32[]{:S(2)}) async-start(bf16[8,64,1024]{2,1,0:T(8,128)(2,1)} %param.11), calls=%async_computation | async-start | bytes 2097152 | tf_op jit(solution)/shard_map/all_to_all | solution.py:85
  6.5 25.0 %all-to-all-done = bf16[8,64,1024]{2,1,0:T(8,128)(2,1)S(1)} async-done(((bf16[8,64,1024]{2,1,0:T(8,128)(2,1)}), bf16[8,64,1024]{2,1,0:T(8,128)(2,1)S(1)}, u32[]{:S(2)}, u32[]{:S(2)}) %all-to-all-start) | async-done | bytes 1048608 | tf_op jit(solution)/shard_map/all_to_all | solution.py:85
  32.1 1.3 copy-done.3
  33.7 1.7 copy-done.11
  35.4 3.5 %fusion.64 = f32[512,3072]{1,0:T(8,128)S(1)} fusion(bf16[512,1024]{1,0:T(8,128)(2,1)S(1)} %fusion.2, bf16[1024,3072]{1,0:T(8,128)(2,1)S(1)} %copy-done.11), kind=kOutput, calls=%fused_computation.111 | convolution fusion | flops 3221225472 | bytes 13631488 | tf_op jit(solution)/shard_map/dot_general | solution.py:22
  39.0 3.9 %slice_multiply_fusion.2 = (f32[512,1024]{1,0:T(8,128)}, f32[512,1024]{1,0:T(8,128)}, f32[64,8,8,128]{3,1,2,0:T(8,128)}, f32[64,8,8,128]{3,1,2,0:T(8,128)}) fusion(f32[512,3072]{1,0:T(8,128)S(1)} %fusion.64), kind=kLoop, calls=%fused_computation.53 | loop fusion | flops 1048576 | bytes 12582912 | tf_op jit(solution)/shard_map/mul | solution.py:28
  42.9 1.2 copy.163
  44.1 1.6 copy.129
  45.8 2.9 %copy.122 = f32[512,1024]{0,1:T(8,128)} copy(f32[512,1024]{1,0:T(8,128)} %get-tuple-element.6) | data formatting | bytes 4194304 | tf_op jit(solution)/shard_map/mul | solution.py:28
  48.7 1.9 bitcast_reduce_fusion.3
  50.6 1.6 mul.154
  52.1 3.6 %mul.155 = f32[2,256,8,128]{1,0,3,2:T(2,128)} reshape(f32[512,16,64]{0,2,1:T(8,128)} %mul.154) | data formatting | bytes 4194304 | tf_op jit(solution)/shard_map/mul | solution.py:27
  55.7 2.9 %copy.125 = f32[512,1024]{0,1:T(8,128)} copy(f32[512,1024]{1,0:T(8,128)} %get-tuple-element.7) | data formatting | bytes 4194304 | tf_op jit(solution)/shard_map/mul | solution.py:31
  58.6 1.9 bitcast_reduce_fusion.2
  60.5 1.6 mul.164
  62.0 3.5 %mul.165 = f32[2,256,8,128]{1,0,3,2:T(2,128)} reshape(f32[512,16,64]{0,2,1:T(8,128)} %mul.164) | data formatting | bytes 4194304 | tf_op jit(solution)/shard_map/mul | solution.py:31
  65.5 3.4 %copy.164 = f32[64,8,8,128]{3,2,1,0:T(8,128)} copy(f32[64,8,8,128]{3,1,2,0:T(8,128)} %get-tuple-element.8) | data formatting | bytes 4194304
  68.9 2.9 %copy.126 = f32[2,256,8,128]{1,0,3,2:T(2,128)} copy(f32[2,256,8,128]{3,2,1,0:T(8,128)} %bitcast.175) | data formatting | bytes 4194304 | tf_op jit(solution)/shard_map/reshape | solution.py:24
  71.8 4.3 %fusion.27 = bf16[2,8,256,128]{2,0,3,1:T(2,128)(2,1)} fusion(f32[2,256,8,128]{1,0,3,2:T(2,128)} %copy.126, f32[2,256,8,128]{1,0,3,2:T(2,128)} %mul.165), kind=kLoop, calls=%fused_computation.58 | loop fusion | flops 1048576 | bytes 5242880 | tf_op jit(solution)/shard_map/transpose | solution.py:42
  76.1 3.6 %copy.128 = bf16[2,8,256,128]{3,2,1,0:T(8,128)(2,1)} copy(bf16[2,8,256,128]{2,0,3,1:T(2,128)(2,1)} %fusion.27) | data formatting | bytes 2097152 | tf_op jit(solution)/shard_map/transpose | solution.py:42
  79.7 3.4 %copy.165 = f32[64,8,8,128]{3,2,1,0:T(8,128)} copy(f32[64,8,8,128]{3,1,2,0:T(8,128)} %get-tuple-element.9) | data formatting | bytes 4194304
  83.1 2.9 %copy.123 = f32[2,256,8,128]{1,3,2,0:T(8,128)} copy(f32[2,256,8,128]{3,2,1,0:T(8,128)} %bitcast.176) | data formatting | bytes 4194304 | tf_op jit(solution)/shard_map/reshape | solution.py:23
  86.0 2.6 %fusion.19 = bf16[2,256,8,128]{1,3,2,0:T(8,128)(2,1)S(1)} fusion(f32[2,256,8,128]{1,3,2,0:T(8,128)} %copy.123, f32[2,256,8,128]{1,0,3,2:T(2,128)} %mul.155, f32[8,128]{1,0:T(8,128)S(1)} %mul.159), kind=kLoop, calls=%fused_computation.40 | loop fusion | flops 1572864 | bytes 5246976 | tf_op jit(solution)/shard_map/convert_element_type | solution.py:33
  92.3 1.3 fusion.3
  93.6 1.1 copy.135
  94.7 27.3 %all_to_all.54 = bf16[2,256,1024]{2,0,1:T(2,128)(2,1)S(1)} all-to-all(bf16[2,256,1024]{2,0,1:T(2,128)(2,1)S(1)} %copy.135), channel_id=1, replica_groups=mesh['tm'=8,'patch'=4] {'patch'}, dimensions={1} | all-to-all | bytes 2097152 | tf_op jit(solution)/shard_map/all_to_all | solution.py:93
  122.3 1.5 copy.138
  123.9 5.6 %all-to-all-start.2 = ((bf16[8,64,1024]{2,0,1:T(8,128)(2,1)}), bf16[8,64,1024]{2,0,1:T(8,128)(2,1)S(1)}, u32[]{:S(2)}, u32[]{:S(2)}) async-start(bf16[8,64,1024]{2,0,1:T(8,128)(2,1)} %copy.138), calls=%async_computation.2 | async-start | bytes 2097152 | tf_op jit(solution)/shard_map/all_to_all | solution.py:94
  129.7 11.7 %all-to-all-done.2 = bf16[8,64,1024]{2,0,1:T(8,128)(2,1)S(1)} async-done(((bf16[8,64,1024]{2,0,1:T(8,128)(2,1)}), bf16[8,64,1024]{2,0,1:T(8,128)(2,1)S(1)}, u32[]{:S(2)}, u32[]{:S(2)}) %all-to-all-start.2) | async-done | bytes 1048608 | tf_op jit(solution)/shard_map/all_to_all | solution.py:94
  142.0 1.2 fusion.10
  143.2 1.3 fusion.12
  144.5 5.5 %fusion.65 = f32[512,3072]{1,0:T(8,128)S(1)} fusion(bf16[512,1024]{1,0:T(8,128)(2,1)S(1)} %bitcast.183, bf16[1024,3072]{1,0:T(8,128)(2,1)} %param.18), kind=kOutput, calls=%fused_computation.112 | convolution fusion | flops 3221225472 | bytes 13631488 | tf_op jit(solution)/shard_map/dot_general | solution.py:22
  150.2 3.1 %slice_bitcast_fusion = (f32[64,8,8,128]{3,1,2,0:T(8,128)S(1)}, f32[512,1024]{1,0:T(8,128)}, f32[512,1024]{1,0:T(8,128)}, f32[64,8,8,128]{3,1,2,0:T(8,128)}) fusion(f32[512,3072]{1,0:T(8,128)S(1)} %fusion.65), kind=kLoop, calls=%fused_computation.50 | loop fusion | flops 1048576 | bytes 12582912
  153.3 1.8 copy.167
  155.1 3.0 %copy.141 = f32[512,1024]{0,1:T(8,128)} copy(f32[512,1024]{1,0:T(8,128)} %get-tuple-element.3) | data formatting | bytes 4194304 | tf_op jit(solution)/shard_map/mul | solution.py:28
  158.1 1.9 bitcast_reduce_fusion.1
  160.1 2.9 %copy.145 = f32[512,1024]{0,1:T(8,128)} copy(f32[512,1024]{1,0:T(8,128)} %get-tuple-element.4) | data formatting | bytes 4194304 | tf_op jit(solution)/shard_map/mul | solution.py:31
  163.0 1.9 bitcast_reduce_fusion
  165.7 3.4 %copy.166 = f32[64,8,8,128]{3,2,1,0:T(8,128)} copy(f32[64,8,8,128]{3,1,2,0:T(8,128)} %get-tuple-element.5) | data formatting | bytes 4194304
  169.2 2.5 %mul.184 = f32[512,16,64]{2,1,0:T(8,128)} broadcast(f32[512,16]{1,0:T(8,128)S(1)} %copy-done.6), dimensions={0,1} | broadcast | bytes 2129920 | tf_op jit(solution)/shard_map/mul | solution.py:31
  171.7 4.6 %mul.185 = f32[8,64,8,128]{3,2,1,0:T(8,128)} reshape(f32[512,16,64]{2,1,0:T(8,128)} %mul.184) | data formatting | bytes 4194304 | tf_op jit(solution)/shard_map/mul | solution.py:31
  176.3 2.5 %mul.174 = f32[512,16,64]{2,1,0:T(8,128)} broadcast(f32[512,16]{1,0:T(8,128)S(1)} %copy.142), dimensions={0,1} | broadcast | bytes 2129920 | tf_op jit(solution)/shard_map/mul | solution.py:27
  178.9 4.6 %mul.175 = f32[8,64,8,128]{3,2,1,0:T(8,128)} reshape(f32[512,16,64]{2,1,0:T(8,128)} %mul.174) | data formatting | bytes 4194304 | tf_op jit(solution)/shard_map/mul | solution.py:27
  183.5 2.6 %fusion.30 = bf16[8,8,64,128]{3,1,2,0:T(8,128)(2,1)S(1)} fusion(f32[8,64,8,128]{3,2,1,0:T(8,128)} %mul.185, f32[8,64,8,128]{3,2,1,0:T(8,128)} %bitcast.173), kind=kLoop, calls=%fused_computation.61 | loop fusion | flops 1048576 | bytes 5242880 | tf_op jit(solution)/shard_map/transpose | solution.py:42
  190.0 1.9 fusion.26
  192.0 2.1 fusion.6
  194.7 20.1 %all_to_all.55 = bf16[64,8,1024]{2,1,0:T(8,128)(2,1)S(1)} all-to-all(bf16[64,8,1024]{2,1,0:T(8,128)(2,1)S(1)} %copy.153), channel_id=1, replica_groups=mesh['tm'=8,'patch'=4] {'tm'}, dimensions={0} | all-to-all | bytes 2097152 | tf_op jit(solution)/shard_map/all_to_all | solution.py:107
  214.9 2.3 %subtract_convert_fusion = bf16[8,64,1024]{2,1,0:T(8,128)(2,1)} fusion(bf16[8,64,1024]{2,1,0:T(8,128)(2,1)S(1)} %bitcast.184, bf16[1024,1024]{1,0:T(8,128)(2,1)S(1)} %copy-done.13, s32[8,64]{1,0:T(8,128)S(1)} %copy-done.14), kind=kOutput, calls=%fused_computation.41 | convolution fusion | flops 1075838976 | bytes 4196352 | tf_op jit(solution)/shard_map/dot_general | solution.py:110
  (71 shorter events, 11.9 us)
Async XLA Ops:
  0.6 91.0 %copy-start = (bf16[1024,1024]{1,0:T(8,128)(2,1)S(1)}, bf16[1024,1024]{1,0:T(8,128)(2,1)}, u32[]{:S(2)}) copy-start(bf16[1024,1024]{1,0:T(8,128)(2,1)} %param.15) | copy-start | bytes 6291460
  0.6 5.6 %copy-start.15 = (f32[16]{0:T(128)S(1)}, f32[16]{0:T(128)}, u32[]{:S(2)}) copy-start(f32[16]{0:T(128)} %param.16) | copy-start | bytes 196
  0.7 30.8 %all-to-all-start = ((bf16[8,64,1024]{2,1,0:T(8,128)(2,1)}), bf16[8,64,1024]{2,1,0:T(8,128)(2,1)S(1)}, u32[]{:S(2)}, u32[]{:S(2)}) async-start(bf16[8,64,1024]{2,1,0:T(8,128)(2,1)} %param.11), calls=%async_computation | async-start | bytes 2097152 | tf_op jit(solution)/shard_map/all_to_all | solution.py:85
  6.5 27.0 %copy-start.9 = (f32[1024]{0:T(1024)S(1)}, f32[1024]{0:T(1024)}, u32[]{:S(2)}) copy-start(f32[1024]{0:T(1024)} %param.13) | copy-start | bytes 12292
  31.8 3.5 %copy-start.11 = (bf16[1024,3072]{1,0:T(8,128)(2,1)S(1)}, bf16[1024,3072]{1,0:T(8,128)(2,1)}, u32[]{:S(2)}) copy-start(bf16[1024,3072]{1,0:T(8,128)(2,1)} %param.14) | copy-start | bytes 18874372
  32.1 1.4 copy-start.3
  86.0 2.6 %copy-start.7 = (bf16[2,8,256,128]{3,2,1,0:T(8,128)(2,1)S(1)}, bf16[2,8,256,128]{3,2,1,0:T(8,128)(2,1)}, u32[]{:S(2)}) copy-start(bf16[2,8,256,128]{3,2,1,0:T(8,128)(2,1)} %copy.128) | copy-start | bytes 3145732
  90.7 1.6 copy-start.4
  122.3 7.2 %copy-start.16 = (f32[16]{0:T(128)S(1)}, f32[16]{0:T(128)}, u32[]{:S(2)}) copy-start(f32[16]{0:T(128)} %param.20) | copy-start | bytes 196
  123.9 17.5 %all-to-all-start.2 = ((bf16[8,64,1024]{2,0,1:T(8,128)(2,1)}), bf16[8,64,1024]{2,0,1:T(8,128)(2,1)S(1)}, u32[]{:S(2)}, u32[]{:S(2)}) async-start(bf16[8,64,1024]{2,0,1:T(8,128)(2,1)} %copy.138), calls=%async_computation.2 | async-start | bytes 2097152 | tf_op jit(solution)/shard_map/all_to_all | solution.py:94
  129.7 13.5 %copy-start.10 = (f32[1024]{0:T(1024)S(1)}, f32[1024]{0:T(1024)}, u32[]{:S(2)}) copy-start(f32[1024]{0:T(1024)} %param.17) | copy-start | bytes 12292
  165.7 3.4 %copy-start.6 = (f32[512,16]{1,0:T(8,128)S(1)}, f32[512,16]{1,0:T(8,128)}, u32[]{:S(2)}) copy-start(f32[512,16]{1,0:T(8,128)} %copy.146) | copy-start | bytes 98308
  183.5 2.9 %copy-start.2 = (f32[8,64,8,128]{3,2,1,0:T(8,128)S(1)}, f32[8,64,8,128]{3,2,1,0:T(8,128)}, u32[]{:S(2)}) copy-start(f32[8,64,8,128]{3,2,1,0:T(8,128)} %mul.175) | copy-start | bytes 6291460
  183.5 3.5 %copy-start.5 = (f32[64,8,8,128]{3,2,1,0:T(8,128)S(1)}, f32[64,8,8,128]{3,2,1,0:T(8,128)}, u32[]{:S(2)}) copy-start(f32[64,8,8,128]{3,2,1,0:T(8,128)} %copy.166) | copy-start | bytes 6291460
  190.0 2.0 copy-start.12
  194.7 20.2 %copy-start.13 = (bf16[1024,1024]{1,0:T(8,128)(2,1)S(1)}, bf16[1024,1024]{1,0:T(8,128)(2,1)}, u32[]{:S(2)}) copy-start(bf16[1024,1024]{1,0:T(8,128)(2,1)} %param.21) | copy-start | bytes 6291460
  194.7 20.2 %copy-start.14 = (s32[8,64]{1,0:T(8,128)S(1)}, s32[8,64]{1,0:T(8,128)}, u32[]{:S(2)}) copy-start(s32[8,64]{1,0:T(8,128)} %param.12) | copy-start | bytes 6148
  214.8 2.3 %copy-start.8 = (bf16[8,8,8,1024]{3,2,0,1:T(8,128)(2,1)}, bf16[8,8,8,1024]{3,2,0,1:T(8,128)(2,1)S(1)}, u32[]{:S(2)}) copy-start(bf16[8,8,8,1024]{3,2,0,1:T(8,128)(2,1)S(1)} %copy.205) | copy-start | bytes 3145732
  214.9 2.3 %copy-start.1 = (bf16[1024,1024]{1,0:T(8,128)(2,1)S(1)}, bf16[1024,1024]{1,0:T(8,128)(2,1)}, u32[]{:S(2)}) copy-start(bf16[1024,1024]{1,0:T(8,128)(2,1)} %param.15) | copy-start | bytes 6291460
where the time goes:
time: 220 us; the launch traced here: 217 us
  local copies, waits for them, and re-layouts  71.2 us (32%)
  blocking collectives  47.3 us (22%)
  waiting for transfers between devices  36.6 us (17%)
  other arithmetic  28.3 us (13%)
  matrix products  21.5 us (10%)
  starting transfers between devices  11.2 us (5%)
    all_to_all x1, blocking collectives, shards(): lax.all_to_all(stream, 'patch', split_axis=1, concat_axis=0, tiled=True)  27.3 us
    all_to_all x1, waiting for transfers between devices, shards(): lax.all_to_all(frames_in, 'patch', split_axis=0, concat_axis=1, tiled=True)  25 us
    all_to_all x1, blocking collectives, shards(): lax.all_to_all(output, 'tm', split_axis=0, concat_axis=1, tiled=True)  20.1 us
    unnamed x42, local copies, waits for them, and re-layouts  18.6 us
    mul x6, local copies, waits for them, and re-layouts, project(): key = key * lax.rsqrt(jnp.mean(key * key, -1, keepdims=True) + 1e-06)  18 us
    mul x10, local copies, waits for them, and re-layouts, project(): query * lax.rsqrt(jnp.mean(query * query, -1, keepdims=True) + 1e-06)  12.7 us
    all_to_all x1, waiting for transfers between devices, shards(): lax.all_to_all(stream, 'tm', split_axis=1, concat_axis=0, tiled=True)  11.7 us
    dot_general x2, matrix products, project(): jnp.dot(normed.reshape(-1, width), weights, preferred_element_type=jnp.fl...  8.99 us
  transfers between devices with their start and end apart: 2, of which 2 were waited for; matrix products, arithmetic and copies ran while one was open for 0% of the time, Pallas kernels for 0%

commit v1 on v0

v1 whole, which is shorter than its diff:
```python
import functools

import jax
import jax.numpy as jnp
from jax import lax
from jax.experimental import pallas as pl
from jax.experimental.pallas import tpu as pltpu
from jax.sharding import PartitionSpec as P

HD = 64
LANES = 256
PACK = 16
MESH = pl.DeviceIdType.MESH


def lane_heads(rows):
    return lax.broadcasted_iota(jnp.int32, (rows, LANES), 1) // HD


def attend(x, gain, qkv_ref, out_ref, scale_ref, allowed, normed, attn):
    count, width = x.shape
    heads = LANES // HD
    square = jnp.mean(x * x, -1, keepdims=True)
    normed[...] = (x * lax.rsqrt(square + 1e-05) * gain).astype(jnp.bfloat16)
    lane_head = lane_heads(1)
    own_head = lax.broadcasted_iota(jnp.int32, (LANES, LANES), 0) // HD == lane_heads(LANES)
    head_mean = jnp.where(own_head, 1.0 / HD, 0.0).astype(jnp.bfloat16)
    rows_head = lax.broadcasted_iota(jnp.int32, (heads * count, LANES), 0) // count
    head_sum = jnp.where(rows_head == lane_heads(heads * count), 1.0, 0.0).astype(jnp.bfloat16)

    def unit(part):
        mean = jnp.dot(
            (part * part).astype(jnp.bfloat16), head_mean, preferred_element_type=jnp.float32
        )
        return part * lax.rsqrt(mean + 1e-06)

    def group(g, carry):
        def project(block):
            columns = pl.ds(pl.multiple_of(block * width + g * LANES, LANES), LANES)
            return jnp.dot(normed[...], qkv_ref[:, columns], preferred_element_type=jnp.float32)

        scale = jnp.zeros((1, LANES), jnp.float32)
        for h in range(heads):
            scale = jnp.where(lane_head == h, scale_ref[g * heads + h], scale)
        query = unit(project(0)) * (scale * (1.0 / HD))
        key = unit(project(1)).astype(jnp.bfloat16)
        value = project(2)
        stacked = jnp.concatenate(
            [jnp.where(lane_head == h, query, 0.0).astype(jnp.bfloat16) for h in range(heads)], 0
        )
        values = jnp.concatenate(
            [jnp.where(lane_head == h, value, 0.0).astype(jnp.bfloat16) for h in range(heads)], 0
        )
        scores = lax.dot_general(
            stacked, key, (((1,), (1,)), ((), ())), preferred_element_type=jnp.float32
        )
        weights = []
        for h in range(heads):
            weight = jnp.exp(scores[h * count : (h + 1) * count])
            if allowed is not None:
                weight = jnp.where(allowed, weight, 0.0)
            weights.append(weight.astype(jnp.bfloat16))
        weight = jnp.concatenate(weights, 1)
        total = jnp.dot(weight, values, preferred_element_type=jnp.float32)
        denom = jnp.dot(weight, head_sum, preferred_element_type=jnp.float32)
        columns = pl.ds(pl.multiple_of(g * LANES, LANES), LANES)
        attn[:, columns] = (total / denom).astype(jnp.bfloat16)
        return carry

    lax.fori_loop(0, width // LANES, group, 0)
    return x + jnp.dot(attn[...], out_ref[...], preferred_element_type=jnp.float32)


def kernel(
    n_tm,
    n_patch,
    x_hbm,
    codes_ref,
    gain_space,
    qkv_space_hbm,
    out_space_hbm,
    scale_space,
    gain_time,
    qkv_time_hbm,
    out_time_hbm,
    scale_time,
    codebook_hbm,
    encoded,
    commitment,
    qkv_space,
    out_space,
    qkv_time,
    out_time,
    codebook,
    whole,
    packed,
    arrived,
    wide,
    leaving,
    landed,
    chosen,
    normed_s,
    attn_s,
    normed_t,
    attn_t,
    load_sem,
    in_send,
    in_recv,
    mid_send,
    mid_recv,
    out_send,
    out_recv,
):
    f_local, p_local, width = x_hbm.shape
    f_own, count = whole.shape[:2]
    pt = p_local // n_tm
    pieces = PACK // pt
    piece = width // pieces
    n = n_tm * n_patch
    frames = f_local * n_tm
    i = lax.axis_index("tm")
    j = lax.axis_index("patch")
    me = j * n_tm + i

    barrier = pltpu.get_barrier_semaphore()

    def greet(k, carry):
        other = lax.rem(me + k, n)
        pl.semaphore_signal(
            barrier,
            inc=1,
            device_id=(lax.rem(other, n_tm), other // n_tm),
            device_id_type=MESH,
        )
        return carry

    lax.fori_loop(1, n, greet, 0)
    sources = (qkv_space_hbm, out_space_hbm, qkv_time_hbm, out_time_hbm, codebook_hbm)
    targets = (qkv_space, out_space, qkv_time, out_time, codebook)
    loads = [
        pltpu.make_async_copy(source, target, load_sem.at[k])
        for k, (source, target) in enumerate(zip(sources, targets))
    ]
    pl.semaphore_wait(barrier, n - 1)

    rows = pl.ds(pl.multiple_of(j * p_local, p_local), p_local)
    for f in range(f_own):
        for k in range(1, n_patch):
            to = lax.rem(j + k, n_patch)
            pltpu.make_async_remote_copy(
                src_ref=x_hbm.at[to * f_own + f],
                dst_ref=whole.at[f, rows],
                send_sem=in_send,
                recv_sem=in_recv.at[f],
                device_id=(i, to),
                device_id_type=MESH,
            ).start()
        pltpu.make_async_copy(x_hbm.at[j * f_own + f], whole.at[f, rows], in_recv.at[f]).start()
    for k in (4, 0, 1, 2, 3):
        loads[k].start()

    loads[4].wait()
    code_columns = jnp.transpose(codes_ref[...].astype(jnp.float32))
    code_ids = lax.broadcasted_iota(jnp.int32, (p_local, codebook.shape[0]), 1).astype(jnp.float32)
    for f in range(f_local):
        one_hot = jnp.where(code_columns[:, f : f + 1] == code_ids, 1.0, 0.0).astype(jnp.bfloat16)
        chosen[f] = jnp.dot(
            one_hot, codebook[...], preferred_element_type=jnp.float32
        ).astype(jnp.bfloat16)

    loads[0].wait()
    loads[1].wait()
    for f in range(f_own):
        pltpu.make_async_copy(whole.at[f], whole.at[f], in_recv.at[f]).wait()
        stream = attend(
            whole[f].astype(jnp.float32),
            gain_space[...],
            qkv_space,
            out_space,
            scale_space,
            None,
            normed_s,
            attn_s,
        )
        blocks = stream.reshape(n, pt, width)
        packed[f] = jnp.concatenate(
            [blocks[:, :, c * piece : (c + 1) * piece] for c in range(pieces)], 1
        ).astype(jnp.bfloat16)
        frame = i * f_local + j * f_own + f

        def send(k, carry):
            other = lax.rem(me + k, n)
            pltpu.make_async_remote_copy(
                src_ref=packed.at[f, other],
                dst_ref=arrived.at[frame],
                send_sem=mid_send,
                recv_sem=mid_recv,
                device_id=(lax.rem(other, n_tm), other // n_tm),
                device_id_type=MESH,
            ).start()
            return carry

        lax.fori_loop(1, n, send, 0)
        pltpu.make_async_copy(packed.at[f, me], arrived.at[frame], mid_recv).start()

    loads[2].wait()
    loads[3].wait()
    pltpu.make_async_copy(arrived, arrived, mid_recv).wait()
    for c in range(pieces):
        wide[:, :, c * piece : (c + 1) * piece] = arrived[:, c * pt : (c + 1) * pt, :].astype(
            jnp.float32
        )
    together = max(1, min(pt, LANES // frames))
    size = together * frames
    row = lax.broadcasted_iota(jnp.int32, (size, size), 0)
    column = lax.broadcasted_iota(jnp.int32, (size, size), 1)
    allowed = (row // frames == column // frames) & (row >= column)
    for first in range(0, pt, together):
        x = jnp.concatenate([wide[:, p, :] for p in range(first, first + together)], 0)
        result = attend(
            x, gain_time[...], qkv_time, out_time, scale_time, allowed, normed_t, attn_t
        )
        for p in range(together):
            wide[:, first + p, :] = result[p * frames : (p + 1) * frames]
    for k in range(n_tm):
        leaving[k] = (
            wide[k * f_local : (k + 1) * f_local].reshape(f_local * pt, width).astype(jnp.bfloat16)
        )

    def send_back(k, carry):
        to = lax.rem(i + k, n_tm)
        pltpu.make_async_remote_copy(
            src_ref=leaving.at[to],
            dst_ref=landed.at[i],
            send_sem=out_send,
            recv_sem=out_recv,
            device_id=(to, j),
            device_id_type=MESH,
        ).start()
        return carry

    lax.fori_loop(1, n_tm, send_back, 0)
    pltpu.make_async_copy(leaving.at[i], landed.at[i], out_recv).start()
    pltpu.make_async_copy(landed, landed, out_recv).wait()
    for first in range(0, n_tm, pieces):
        output = jnp.concatenate(
            [
                landed[first + k].astype(jnp.float32).reshape(f_local, pt, width)
                for k in range(pieces)
            ],
            1,
        )
        part = pl.ds(first * pt, PACK)
        encoded[:, part, :] = output.astype(jnp.bfloat16)
        commitment[:, part, :] = (output - chosen[:, part, :].astype(jnp.float32)).astype(
            jnp.bfloat16
        )

    sent = x_hbm.at[pl.ds(0, f_local - f_own)]
    pltpu.make_async_copy(sent, sent, in_send).wait()
    sent = packed.at[:, pl.ds(0, n - 1)]
    pltpu.make_async_copy(sent, sent, mid_send).wait()
    sent = leaving.at[pl.ds(0, n_tm - 1)]
    pltpu.make_async_copy(sent, sent, out_send).wait()


def solution(mesh):
    n_tm, n_patch = mesh.shape["tm"], mesh.shape["patch"]
    n = n_tm * n_patch

    def shards(x, codes, g_s, w_s, o_s, s_s, g_t, w_t, o_t, s_t, book):
        f_local, p_local, width = x.shape
        f_own, count = f_local // n_patch, p_local * n_patch
        frames, pt = f_local * n_tm, p_local // n_tm
        pieces = PACK // pt
        size = max(1, min(pt, LANES // frames)) * frames
        any_space = pl.BlockSpec(memory_space=pl.ANY)
        vmem = pl.BlockSpec(memory_space=pltpu.VMEM)
        smem = pl.BlockSpec(memory_space=pltpu.SMEM)
        bf16, f32 = jnp.bfloat16, jnp.float32
        return pl.pallas_call(
            functools.partial(kernel, n_tm, n_patch),
            out_shape=[jax.ShapeDtypeStruct(x.shape, bf16)] * 2,
            in_specs=[
                any_space,
                vmem,
                vmem,
                any_space,
                any_space,
                smem,
                vmem,
                any_space,
                any_space,
                smem,
                any_space,
            ],
            out_specs=[vmem, vmem],
            scratch_shapes=[
                pltpu.VMEM(w_s.shape, bf16),
                pltpu.VMEM(o_s.shape, bf16),
                pltpu.VMEM(w_t.shape, bf16),
                pltpu.VMEM(o_t.shape, bf16),
                pltpu.VMEM(book.shape, bf16),
                pltpu.VMEM((f_own, count, width), bf16),
                pltpu.VMEM((f_own, n, PACK, width // pieces), bf16),
                pltpu.VMEM((frames, PACK, width // pieces), bf16),
                pltpu.VMEM((frames, pt, width), f32),
                pltpu.VMEM((n_tm, f_local * pt, width), bf16),
                pltpu.VMEM((n_tm, f_local * pt, width), bf16),
                pltpu.VMEM(x.shape, bf16),
                pltpu.VMEM((count, width), bf16),
                pltpu.VMEM((count, width), bf16),
                pltpu.VMEM((size, width), bf16),
                pltpu.VMEM((size, width), bf16),
                pltpu.SemaphoreType.DMA((5,)),
                pltpu.SemaphoreType.DMA,
                pltpu.SemaphoreType.DMA((f_own,)),
                pltpu.SemaphoreType.DMA,
                pltpu.SemaphoreType.DMA,
                pltpu.SemaphoreType.DMA,
                pltpu.SemaphoreType.DMA,
            ],
            compiler_params=pltpu.CompilerParams(
                collective_id=0, has_side_effects=True, vmem_limit_bytes=56 * 1024 * 1024
            ),
            cost_estimate=pl.CostEstimate(
                flops=12_000_000_000, bytes_accessed=24_000_000, transcendentals=4_000_000
            ),
        )(
            x,
            codes,
            g_s.reshape(1, -1),
            w_s,
            o_s,
            s_s,
            g_t.reshape(1, -1),
            w_t,
            o_t,
            s_t,
            book,
        )

    return jax.shard_map(
        shards,
        mesh=mesh,
        in_specs=(P("tm", "patch", None), P("tm", "patch")) + (P(),) * 9,
        out_specs=(P("tm", "patch", None), P("tm", "patch", None)),
        check_vma=False,
    )
```

time: 220 us -> 86.1 us (0.39)
  Pallas kernels: 0 us -> 80.6 us
  local copies, waits for them, and re-layouts: 71.2 us -> 3.32 us
  blocking collectives: 47.3 us -> 0 us
  waiting for transfers between devices: 36.6 us -> 0 us
  other arithmetic: 28.3 us -> 0 us
  matrix products: 21.5 us -> 0 us
  starting transfers between devices: 11.2 us -> 0 us
    pallas_call x0 -> x1, Pallas kernels: none -> 80.6 us  [shards(): pl.pallas_call(functools.partial(kernel, n_tm, n_patch), out_shape=[jax.S...]
    all_to_all x2 -> x0, blocking collectives: 47.3 us -> none  [the longest x1 27.3 us: shards(): lax.all_to_all(stream, 'patch', split_axis=1, concat_axis=0, tiled=True)]
    all_to_all x2 -> x0, waiting for transfers between devices: 36.6 us -> none  [the longest x1 25 us: shards(): lax.all_to_all(frames_in, 'patch', split_axis=0, concat_axis=1, tiled=True)]
    mul x18 -> x0, local copies, waits for them, and re-layouts: 36.6 us -> none  [the longest x6 18 us: project(): key = key * lax.rsqrt(jnp.mean(key * key, -1, keepdims=True) + 1e-06)]
    dot_general x13 -> x0, matrix products: 21.5 us -> none  [the longest x2 8.99 us: project(): jnp.dot(normed.reshape(-1, width), weights, preferred_element_type=jnp.fl...]
    unnamed x42 -> x4, local copies, waits for them, and re-layouts: 18.6 us -> 3.32 us
    all_to_all x2 -> x0, starting transfers between devices: 11.2 us -> none  [the longest x1 5.6 us: shards(): lax.all_to_all(stream, 'tm', split_axis=1, concat_axis=0, tiled=True)]
    reduce_sum x6 -> x0, other arithmetic: 8.96 us -> none  [the longest x2 3.76 us: project(): jnp.mean(query * query, -1, keepdims=True) + 1e-06]
  transfers between devices with their start and end apart: 2 -> 0, of which waited for: 2 -> 0; matrix products, arithmetic and copies ran while one was open for 0% -> 0% of each run, Pallas kernels for 0% -> 0%
where the time goes in v1:
time: 86.1 us; the launch traced here: 84.6 us
  Pallas kernels  80.6 us (94%)
  local copies, waits for them, and re-layouts  3.32 us (4%)
    pallas_call x1, Pallas kernels, shards(): pl.pallas_call(functools.partial(kernel, n_tm, n_patch), out_shape=[jax.S...  80.6 us
    unnamed x4, local copies, waits for them, and re-layouts  3.32 us

profile of v1, /device:TPU:1, one launch (start us, length us, event | category | flops | bytes accessed | tf_op | source)
XLA Modules:
  0.0 84.6 jit_solution(9903667602345976643)
XLA Ops:
  0.6 80.6 %shard_map.122 = (bf16[8,64,1024]{2,1,0:T(8,128)(2,1)}, bf16[8,64,1024]{2,1,0:T(8,128)(2,1)}) custom-call(bf16[8,64,1024]{2,1,0:T(8,128)(2,1)} %x_hbm.1, s32[8,64]{1,0:T(8,128)} %codes_ref.1, f32[1,1024]{1,0:T(1,128)} %bitcast.2, bf16[1024,3072]{1,0:T(8,128)(2,1)} %qkv_space_hbm.1, bf16[1024,1024]{1,0:T(8,128)(2,1)} %out_space_hbm.1, f32[16]{0:T(128)} %scale_space.1, ...), custom_call_target="tpu_custom_call" | custom-call | flops 12000000000 | bytes 24000000 | tf_op jit(solution)/shard_map/pallas_call | solution.py:281
  81.3 0.0 copy-start
  81.3 2.4 %copy.15 = bf16[8,64,1024]{2,1,0:T(8,128)(2,1)} copy(bf16[8,64,1024]{2,1,0:T(8,128)(2,1)} %get-tuple-element.4) | data formatting | bytes 2097152
  83.6 0.0 copy-done
  83.6 1.0 %copy.16 = bf16[8,64,1024]{2,1,0:T(8,128)(2,1)} copy(bf16[8,64,1024]{2,1,0:T(8,128)(2,1)S(1)} %copy-done) | data formatting | bytes 2097152
Async XLA Ops:
  81.3 2.4 %copy-start = (bf16[8,64,1024]{2,1,0:T(8,128)(2,1)S(1)}, bf16[8,64,1024]{2,1,0:T(8,128)(2,1)}, u32[]{:S(2)}) copy-start(bf16[8,64,1024]{2,1,0:T(8,128)(2,1)} %get-tuple-element.5) | copy-start | bytes 3145732

commit v2 on v1

--- a/solution.py
+++ b/solution.py
@@ -10,6 +10,7 @@
 HD = 64
 LANES = 256
 PACK = 16
+LOG2_E = 1.4426950408889634
 MESH = pl.DeviceIdType.MESH
 
 
@@ -42,7 +43,7 @@
         scale = jnp.zeros((1, LANES), jnp.float32)
         for h in range(heads):
             scale = jnp.where(lane_head == h, scale_ref[g * heads + h], scale)
-        query = unit(project(0)) * (scale * (1.0 / HD))
+        query = unit(project(0)) * (scale * (LOG2_E / HD))
         key = unit(project(1)).astype(jnp.bfloat16)
         value = project(2)
         stacked = jnp.concatenate(
@@ -56,7 +57,7 @@
         )
         weights = []
         for h in range(heads):
-            weight = jnp.exp(scores[h * count : (h + 1) * count])
+            weight = jnp.exp2(scores[h * count : (h + 1) * count])
             if allowed is not None:
                 weight = jnp.where(allowed, weight, 0.0)
             weights.append(weight.astype(jnp.bfloat16))
@@ -67,7 +68,7 @@
         attn[:, columns] = (total / denom).astype(jnp.bfloat16)
         return carry
 
-    lax.fori_loop(0, width // LANES, group, 0)
+    lax.fori_loop(0, width // LANES, group, 0, unroll=2)
     return x + jnp.dot(attn[...], out_ref[...], preferred_element_type=jnp.float32)
 
 
@@ -113,9 +114,9 @@
 ):
     f_local, p_local, width = x_hbm.shape
     f_own, count = whole.shape[:2]
-    pt = p_local // n_tm
-    pieces = PACK // pt
-    piece = width // pieces
+    halves, piece = arrived.shape[0], arrived.shape[3]
+    pg = p_local // n_tm // halves
+    pieces = PACK // pg
     n = n_tm * n_patch
     frames = f_local * n_tm
     i = lax.axis_index("tm")
@@ -144,18 +145,25 @@
     pl.semaphore_wait(barrier, n - 1)
 
     rows = pl.ds(pl.multiple_of(j * p_local, p_local), p_local)
-    for f in range(f_own):
+
+    def share(f):
         for k in range(1, n_patch):
             to = lax.rem(j + k, n_patch)
             pltpu.make_async_remote_copy(
                 src_ref=x_hbm.at[to * f_own + f],
                 dst_ref=whole.at[f, rows],
-                send_sem=in_send,
+                send_sem=in_send.at[f],
                 recv_sem=in_recv.at[f],
                 device_id=(i, to),
                 device_id_type=MESH,
             ).start()
         pltpu.make_async_copy(x_hbm.at[j * f_own + f], whole.at[f, rows], in_recv.at[f]).start()
+
+    def shared(f):
+        sent = x_hbm.at[pl.ds(0, n_patch - 1)]
+        pltpu.make_async_copy(sent, sent, in_send.at[f]).wait()
+
+    share(0)
     for k in (4, 0, 1, 2, 3):
         loads[k].start()
 
@@ -170,6 +178,9 @@
 
     loads[0].wait()
     loads[1].wait()
+    for f in range(1, f_own):
+        shared(f - 1)
+        share(f)
     for f in range(f_own):
         pltpu.make_async_copy(whole.at[f], whole.at[f], in_recv.at[f]).wait()
         stream = attend(
@@ -182,85 +193,98 @@
             normed_s,
             attn_s,
         )
-        blocks = stream.reshape(n, pt, width)
-        packed[f] = jnp.concatenate(
-            [blocks[:, :, c * piece : (c + 1) * piece] for c in range(pieces)], 1
-        ).astype(jnp.bfloat16)
+        blocks = stream.reshape(n * halves, pg, width)
+        packed[f] = (
+            jnp.concatenate([blocks[:, :, c * piece : (c + 1) * piece] for c in range(pieces)], 1)
+            .astype(jnp.bfloat16)
+            .reshape(packed.shape[1:])
+        )
         frame = i * f_local + j * f_own + f
-
-        def send(k, carry):
+        last = f == f_own - 1
+
+        def send(k, carry, half):
             other = lax.rem(me + k, n)
+            to_i, to_j = lax.rem(other, n_tm), other // n_tm
+            part = half if last else slice(None)
             pltpu.make_async_remote_copy(
-                src_ref=packed.at[f, other],
-                dst_ref=arrived.at[frame],
+                src_ref=packed.at[f, to_j, part, to_i],
+                dst_ref=arrived.at[part, frame],
                 send_sem=mid_send,
-                recv_sem=mid_recv,
-                device_id=(lax.rem(other, n_tm), other // n_tm),
+                recv_sem=mid_recv.at[half if last else halves],
+                device_id=(to_i, to_j),
                 device_id_type=MESH,
             ).start()
             return carry
 
-        lax.fori_loop(1, n, send, 0)
-        pltpu.make_async_copy(packed.at[f, me], arrived.at[frame], mid_recv).start()
+        for half in range(halves if last else 1):
+            part = half if last else slice(None)
+            lax.fori_loop(1, n, functools.partial(send, half=half), 0)
+            pltpu.make_async_copy(
+                packed.at[f, j, part, i],
+                arrived.at[part, frame],
+                mid_recv.at[half if last else halves],
+            ).start()
 
     loads[2].wait()
     loads[3].wait()
-    pltpu.make_async_copy(arrived, arrived, mid_recv).wait()
-    for c in range(pieces):
-        wide[:, :, c * piece : (c + 1) * piece] = arrived[:, c * pt : (c + 1) * pt, :].astype(
-            jnp.float32
-        )
-    together = max(1, min(pt, LANES // frames))
-    size = together * frames
-    row = lax.broadcasted_iota(jnp.int32, (size, size), 0)
-    column = lax.broadcasted_iota(jnp.int32, (size, size), 1)
-    allowed = (row // frames == column // frames) & (row >= column)
-    for first in range(0, pt, together):
-        x = jnp.concatenate([wide[:, p, :] for p in range(first, first + together)], 0)
+    row = lax.broadcasted_iota(jnp.int32, (LANES, LANES), 0)
+    column = lax.broadcasted_iota(jnp.int32, (LANES, LANES), 1)
+    allowed = (lax.rem(row, pg) == lax.rem(column, pg)) & (row >= column)
+    if f_own > 1:
+        early = arrived.at[:, pl.ds(0, (f_own - 1) * n)]
+        pltpu.make_async_copy(early, early, mid_recv.at[halves]).wait()
+    for half in range(halves):
+        late = arrived.at[half, pl.ds(0, n)]
+        pltpu.make_async_copy(late, late, mid_recv.at[half]).wait()
+        for c in range(pieces):
+            wide[:, c * piece : (c + 1) * piece] = (
+                arrived[half, :, c * pg : (c + 1) * pg, :]
+                .astype(jnp.float32)
+                .reshape(LANES, piece)
+            )
         result = attend(
-            x, gain_time[...], qkv_time, out_time, scale_time, allowed, normed_t, attn_t
-        )
-        for p in range(together):
-            wide[:, first + p, :] = result[p * frames : (p + 1) * frames]
-    for k in range(n_tm):
-        leaving[k] = (
-            wide[k * f_local : (k + 1) * f_local].reshape(f_local * pt, width).astype(jnp.bfloat16)
-        )
-
-    def send_back(k, carry):
-        to = lax.rem(i + k, n_tm)
-        pltpu.make_async_remote_copy(
-            src_ref=leaving.at[to],
-            dst_ref=landed.at[i],
-            send_sem=out_send,
-            recv_sem=out_recv,
-            device_id=(to, j),
-            device_id_type=MESH,
-        ).start()
-        return carry
-
-    lax.fori_loop(1, n_tm, send_back, 0)
-    pltpu.make_async_copy(leaving.at[i], landed.at[i], out_recv).start()
-    pltpu.make_async_copy(landed, landed, out_recv).wait()
-    for first in range(0, n_tm, pieces):
-        output = jnp.concatenate(
-            [
-                landed[first + k].astype(jnp.float32).reshape(f_local, pt, width)
-                for k in range(pieces)
-            ],
-            1,
-        )
-        part = pl.ds(first * pt, PACK)
-        encoded[:, part, :] = output.astype(jnp.bfloat16)
-        commitment[:, part, :] = (output - chosen[:, part, :].astype(jnp.float32)).astype(
-            jnp.bfloat16
-        )
-
-    sent = x_hbm.at[pl.ds(0, f_local - f_own)]
-    pltpu.make_async_copy(sent, sent, in_send).wait()
-    sent = packed.at[:, pl.ds(0, n - 1)]
-    pltpu.make_async_copy(sent, sent, mid_send).wait()
-    sent = leaving.at[pl.ds(0, n_tm - 1)]
+            wide[...], gain_time[...], qkv_time, out_time, scale_time, allowed, normed_t, attn_t
+        )
+        leaving[half] = result.astype(jnp.bfloat16).reshape(leaving.shape[1:])
+
+        def send_back(k, carry):
+            to = lax.rem(i + k, n_tm)
+            pltpu.make_async_remote_copy(
+                src_ref=leaving.at[half, to],
+                dst_ref=landed.at[half, i],
+                send_sem=out_send,
+                recv_sem=out_recv.at[half],
+                device_id=(to, j),
+                device_id_type=MESH,
+            ).start()
+            return carry
+
+        lax.fori_loop(1, n_tm, send_back, 0)
+        pltpu.make_async_copy(leaving.at[half, i], landed.at[half, i], out_recv.at[half]).start()
+
+    for half in range(halves):
+        pltpu.make_async_copy(landed.at[half], landed.at[half], out_recv.at[half]).wait()
+        for first in range(0, n_tm, pieces):
+            output = jnp.concatenate(
+                [
+                    landed[half, first + k].astype(jnp.float32).reshape(f_local, pg, width)
+                    for k in range(pieces)
+                ],
+                1,
+            )
+            part = pl.ds(half * (p_local // halves) + first * pg, PACK)
+            encoded[:, part, :] = output.astype(jnp.bfloat16)
+            commitment[:, part, :] = (output - chosen[:, part, :].astype(jnp.float32)).astype(
+                jnp.bfloat16
+            )
+
+    shared(f_own - 1)
+    for f in range(f_own):
+        sent = packed.at[f, pl.ds(0, n_patch - 1)]
+        pltpu.make_async_copy(sent, sent, mid_send).wait()
+        sent = packed.at[f, 0, :, pl.ds(0, n_tm - 1)]
+        pltpu.make_async_copy(sent, sent, mid_send).wait()
+    sent = leaving.at[:, pl.ds(0, n_tm - 1)]
     pltpu.make_async_copy(sent, sent, out_send).wait()
 
 
@@ -271,9 +295,10 @@
     def shards(x, codes, g_s, w_s, o_s, s_s, g_t, w_t, o_t, s_t, book):
         f_local, p_local, width = x.shape
         f_own, count = f_local // n_patch, p_local * n_patch
-        frames, pt = f_local * n_tm, p_local // n_tm
-        pieces = PACK // pt
-        size = max(1, min(pt, LANES // frames)) * frames
+        frames = f_local * n_tm
+        pg = max(1, LANES // frames)
+        halves = p_local // n_tm // pg
+        piece = width * pg // PACK
         any_space = pl.BlockSpec(memory_space=pl.ANY)
         vmem = pl.BlockSpec(memory_space=pltpu.VMEM)
         smem = pl.BlockSpec(memory_space=pltpu.SMEM)
@@ -302,23 +327,23 @@
                 pltpu.VMEM(o_t.shape, bf16),
                 pltpu.VMEM(book.shape, bf16),
                 pltpu.VMEM((f_own, count, width), bf16),
-                pltpu.VMEM((f_own, n, PACK, width // pieces), bf16),
-                pltpu.VMEM((frames, PACK, width // pieces), bf16),
-                pltpu.VMEM((frames, pt, width), f32),
-                pltpu.VMEM((n_tm, f_local * pt, width), bf16),
-                pltpu.VMEM((n_tm, f_local * pt, width), bf16),
+                pltpu.VMEM((f_own, n_patch, halves, n_tm, PACK, piece), bf16),
+                pltpu.VMEM((halves, frames, PACK, piece), bf16),
+                pltpu.VMEM((LANES, width), f32),
+                pltpu.VMEM((halves, n_tm, f_local * pg, width), bf16),
+                pltpu.VMEM((halves, n_tm, f_local * pg, width), bf16),
                 pltpu.VMEM(x.shape, bf16),
                 pltpu.VMEM((count, width), bf16),
                 pltpu.VMEM((count, width), bf16),
-                pltpu.VMEM((size, width), bf16),
-                pltpu.VMEM((size, width), bf16),
+                pltpu.VMEM((LANES, width), bf16),
+                pltpu.VMEM((LANES, width), bf16),
                 pltpu.SemaphoreType.DMA((5,)),
-                pltpu.SemaphoreType.DMA,
+                pltpu.SemaphoreType.DMA((f_own,)),
                 pltpu.SemaphoreType.DMA((f_own,)),
                 pltpu.SemaphoreType.DMA,
+                pltpu.SemaphoreType.DMA((halves + 1,)),
                 pltpu.SemaphoreType.DMA,
-                pltpu.SemaphoreType.DMA,
-                pltpu.SemaphoreType.DMA,
+                pltpu.SemaphoreType.DMA((halves,)),
             ],
             compiler_params=pltpu.CompilerParams(
                 collective_id=0, has_side_effects=True, vmem_limit_bytes=56 * 1024 * 1024

time: 86.1 us -> 77.6 us (0.901); the launches traced: 84.6 us -> 77.4 us
  Pallas kernels: 80.6 us -> 73.4 us
    pallas_call x1, Pallas kernels: 80.6 us -> 73.4 us  [shards(): pl.pallas_call(functools.partial(kernel, n_tm, n_patch), out_shape=[jax.S...]
where the time goes in v2:
time: 77.6 us; the launch traced here: 77.4 us
  Pallas kernels  73.4 us (95%)
  local copies, waits for them, and re-layouts  3.32 us (4%)
    pallas_call x1, Pallas kernels, shards(): pl.pallas_call(functools.partial(kernel, n_tm, n_patch), out_shape=[jax.S...  73.4 us
    unnamed x4, local copies, waits for them, and re-layouts  3.32 us

profile of v2, /device:TPU:1, one launch (start us, length us, event | category | flops | bytes accessed | tf_op | source)
XLA Modules:
  0.0 77.4 jit_solution(14456808079929104519)
XLA Ops:
  0.6 73.4 %shard_map.122 = (bf16[8,64,1024]{2,1,0:T(8,128)(2,1)}, bf16[8,64,1024]{2,1,0:T(8,128)(2,1)}) custom-call(bf16[8,64,1024]{2,1,0:T(8,128)(2,1)} %x_hbm.1, s32[8,64]{1,0:T(8,128)} %codes_ref.1, f32[1,1024]{1,0:T(1,128)} %bitcast.2, bf16[1024,3072]{1,0:T(8,128)(2,1)} %qkv_space_hbm.1, bf16[1024,1024]{1,0:T(8,128)(2,1)} %out_space_hbm.1, f32[16]{0:T(128)} %scale_space.1, ...), custom_call_target="tpu_custom_call" | custom-call | flops 12000000000 | bytes 24000000 | tf_op jit(solution)/shard_map/pallas_call | solution.py:306
  74.1 0.0 copy-start
  74.1 2.4 %copy.15 = bf16[8,64,1024]{2,1,0:T(8,128)(2,1)} copy(bf16[8,64,1024]{2,1,0:T(8,128)(2,1)} %get-tuple-element.4) | data formatting | bytes 2097152
  76.4 0.0 copy-done
  76.4 1.0 %copy.16 = bf16[8,64,1024]{2,1,0:T(8,128)(2,1)} copy(bf16[8,64,1024]{2,1,0:T(8,128)(2,1)S(1)} %copy-done) | data formatting | bytes 2097152
Async XLA Ops:
  74.1 2.4 %copy-start = (bf16[8,64,1024]{2,1,0:T(8,128)(2,1)S(1)}, bf16[8,64,1024]{2,1,0:T(8,128)(2,1)}, u32[]{:S(2)}) copy-start(bf16[8,64,1024]{2,1,0:T(8,128)(2,1)} %get-tuple-element.5) | copy-start | bytes 3145732

commit v3 on v2

--- a/solution.py
+++ b/solution.py
@@ -14,61 +14,79 @@
 MESH = pl.DeviceIdType.MESH
 
 
-def lane_heads(rows):
-    return lax.broadcasted_iota(jnp.int32, (rows, LANES), 1) // HD
-
-
-def attend(x, gain, qkv_ref, out_ref, scale_ref, allowed, normed, attn):
+def fill_masks(head_mean, head_sum, head_rows, allowed, pg):
+    heads = LANES // HD
+    row = lax.broadcasted_iota(jnp.int32, (LANES, LANES), 0)
+    column = lax.broadcasted_iota(jnp.int32, (LANES, LANES), 1)
+    head_mean[...] = jnp.where(row // HD == column // HD, 1.0 / HD, 0.0).astype(jnp.bfloat16)
+    count = head_sum.shape[0] // heads
+    wide_column = lax.broadcasted_iota(jnp.int32, (count, LANES), 1)
+    few_columns = lax.broadcasted_iota(jnp.int32, (PACK, LANES), 1)
+    for h in range(heads):
+        head_sum[h * count : (h + 1) * count] = jnp.where(
+            wide_column // HD == h, 1.0, 0.0
+        ).astype(jnp.bfloat16)
+        head_rows[h] = jnp.where(few_columns // HD == h, 1.0, 0.0).astype(jnp.bfloat16)
+    allowed[...] = jnp.where(
+        (lax.rem(row, pg) == lax.rem(column, pg)) & (row >= column), 1.0, 0.0
+    ).astype(jnp.bfloat16)
+
+
+def attend(x, gain, qkv_ref, out_ref, scale_ref, masks, allowed, normed, attn):
+    head_mean, head_sum, head_rows = masks
     count, width = x.shape
     heads = LANES // HD
     square = jnp.mean(x * x, -1, keepdims=True)
     normed[...] = (x * lax.rsqrt(square + 1e-05) * gain).astype(jnp.bfloat16)
-    lane_head = lane_heads(1)
-    own_head = lax.broadcasted_iota(jnp.int32, (LANES, LANES), 0) // HD == lane_heads(LANES)
-    head_mean = jnp.where(own_head, 1.0 / HD, 0.0).astype(jnp.bfloat16)
-    rows_head = lax.broadcasted_iota(jnp.int32, (heads * count, LANES), 0) // count
-    head_sum = jnp.where(rows_head == lane_heads(heads * count), 1.0, 0.0).astype(jnp.bfloat16)
+    lane_head = lax.broadcasted_iota(jnp.int32, (1, LANES), 1) // HD
+    step = head_sum.shape[0] // heads
 
     def unit(part):
         mean = jnp.dot(
-            (part * part).astype(jnp.bfloat16), head_mean, preferred_element_type=jnp.float32
+            (part * part).astype(jnp.bfloat16), head_mean[...], preferred_element_type=jnp.float32
         )
         return part * lax.rsqrt(mean + 1e-06)
 
-    def group(g, carry):
+    def by_head(part):
+        return jnp.concatenate([part * head_rows[h][:1] for h in range(heads)], 0)
+
+    def prepare(g):
         def project(block):
-            columns = pl.ds(pl.multiple_of(block * width + g * LANES, LANES), LANES)
-            return jnp.dot(normed[...], qkv_ref[:, columns], preferred_element_type=jnp.float32)
+            first = block * width + g * LANES
+            return jnp.dot(
+                normed[...], qkv_ref[:, first : first + LANES], preferred_element_type=jnp.float32
+            )
 
         scale = jnp.zeros((1, LANES), jnp.float32)
         for h in range(heads):
             scale = jnp.where(lane_head == h, scale_ref[g * heads + h], scale)
-        query = unit(project(0)) * (scale * (LOG2_E / HD))
+        query = (unit(project(0)) * (scale * (LOG2_E / HD))).astype(jnp.bfloat16)
         key = unit(project(1)).astype(jnp.bfloat16)
-        value = project(2)
-        stacked = jnp.concatenate(
-            [jnp.where(lane_head == h, query, 0.0).astype(jnp.bfloat16) for h in range(heads)], 0
-        )
-        values = jnp.concatenate(
-            [jnp.where(lane_head == h, value, 0.0).astype(jnp.bfloat16) for h in range(heads)], 0
-        )
+        value = project(2).astype(jnp.bfloat16)
+        return by_head(query), key, by_head(value)
+
+    ready = prepare(0)
+    for g in range(width // LANES):
+        stacked, key, values = ready
         scores = lax.dot_general(
             stacked, key, (((1,), (1,)), ((), ())), preferred_element_type=jnp.float32
         )
+        if (g + 1) * LANES < width:
+            ready = prepare(g + 1)
         weights = []
         for h in range(heads):
-            weight = jnp.exp2(scores[h * count : (h + 1) * count])
-            if allowed is not None:
-                weight = jnp.where(allowed, weight, 0.0)
-            weights.append(weight.astype(jnp.bfloat16))
+            weight = jnp.exp2(scores[h * count : (h + 1) * count]).astype(jnp.bfloat16)
+            weights.append(weight if allowed is None else weight * allowed[...])
         weight = jnp.concatenate(weights, 1)
         total = jnp.dot(weight, values, preferred_element_type=jnp.float32)
-        denom = jnp.dot(weight, head_sum, preferred_element_type=jnp.float32)
-        columns = pl.ds(pl.multiple_of(g * LANES, LANES), LANES)
-        attn[:, columns] = (total / denom).astype(jnp.bfloat16)
-        return carry
-
-    lax.fori_loop(0, width // LANES, group, 0, unroll=2)
+        if step == count:
+            sums = head_sum[...]
+        else:
+            sums = jnp.concatenate(
+                [head_sum[h * step : h * step + count] for h in range(heads)], 0
+            )
+        denom = jnp.dot(weight, sums, preferred_element_type=jnp.float32)
+        attn[:, g * LANES : (g + 1) * LANES] = (total / denom).astype(jnp.bfloat16)
     return x + jnp.dot(attn[...], out_ref[...], preferred_element_type=jnp.float32)
 
 
@@ -104,6 +122,10 @@
     attn_s,
     normed_t,
     attn_t,
+    head_mean,
+    head_sum,
+    head_rows,
+    allowed,
     load_sem,
     in_send,
     in_recv,
@@ -167,6 +189,8 @@
     for k in (4, 0, 1, 2, 3):
         loads[k].start()
 
+    fill_masks(head_mean, head_sum, head_rows, allowed, pg)
+    masks = (head_mean, head_sum, head_rows)
     loads[4].wait()
     code_columns = jnp.transpose(codes_ref[...].astype(jnp.float32))
     code_ids = lax.broadcasted_iota(jnp.int32, (p_local, codebook.shape[0]), 1).astype(jnp.float32)
@@ -189,6 +213,7 @@
             qkv_space,
             out_space,
             scale_space,
+            masks,
             None,
             normed_s,
             attn_s,
@@ -227,9 +252,6 @@
 
     loads[2].wait()
     loads[3].wait()
-    row = lax.broadcasted_iota(jnp.int32, (LANES, LANES), 0)
-    column = lax.broadcasted_iota(jnp.int32, (LANES, LANES), 1)
-    allowed = (lax.rem(row, pg) == lax.rem(column, pg)) & (row >= column)
     if f_own > 1:
         early = arrived.at[:, pl.ds(0, (f_own - 1) * n)]
         pltpu.make_async_copy(early, early, mid_recv.at[halves]).wait()
@@ -243,7 +265,16 @@
                 .reshape(LANES, piece)
             )
         result = attend(
-            wide[...], gain_time[...], qkv_time, out_time, scale_time, allowed, normed_t, attn_t
+            wide[...],
+            gain_time[...],
+            qkv_time,
+            out_time,
+            scale_time,
+            masks,
+            allowed,
+            normed_t,
+            attn_t,
+
         )
         leaving[half] = result.astype(jnp.bfloat16).reshape(leaving.shape[1:])
 
@@ -337,6 +368,10 @@
                 pltpu.VMEM((count, width), bf16),
                 pltpu.VMEM((LANES, width), bf16),
                 pltpu.VMEM((LANES, width), bf16),
+                pltpu.VMEM((LANES, LANES), bf16),
+                pltpu.VMEM((LANES // HD * max(count, LANES), LANES), bf16),
+                pltpu.VMEM((LANES // HD, PACK, LANES), bf16),
+                pltpu.VMEM((LANES, LANES), bf16),
                 pltpu.SemaphoreType.DMA((5,)),
                 pltpu.SemaphoreType.DMA((f_own,)),
                 pltpu.SemaphoreType.DMA((f_own,)),

time: 77.6 us -> 76.6 us (0.987)
  Pallas kernels: 73.4 us -> 72.4 us
    pallas_call x1, Pallas kernels: 73.4 us -> 72.4 us  [shards(): pl.pallas_call(functools.partial(kernel, n_tm, n_patch), out_shape=[jax.S...]
where the time goes in v3:
time: 76.6 us; the launch traced here: 76.4 us
  Pallas kernels  72.4 us (95%)
  local copies, waits for them, and re-layouts  3.32 us (4%)
    pallas_call x1, Pallas kernels, shards(): pl.pallas_call(functools.partial(kernel, n_tm, n_patch), out_shape=[jax.S...  72.4 us
    unnamed x4, local copies, waits for them, and re-layouts  3.32 us

profile of v3, /device:TPU:1, one launch (start us, length us, event | category | flops | bytes accessed | tf_op | source)
XLA Modules:
  0.0 76.4 jit_solution(2257180142511236801)
XLA Ops:
  0.6 72.4 %shard_map.122 = (bf16[8,64,1024]{2,1,0:T(8,128)(2,1)}, bf16[8,64,1024]{2,1,0:T(8,128)(2,1)}) custom-call(bf16[8,64,1024]{2,1,0:T(8,128)(2,1)} %x_hbm.1, s32[8,64]{1,0:T(8,128)} %codes_ref.1, f32[1,1024]{1,0:T(1,128)} %bitcast.2, bf16[1024,3072]{1,0:T(8,128)(2,1)} %qkv_space_hbm.1, bf16[1024,1024]{1,0:T(8,128)(2,1)} %out_space_hbm.1, f32[16]{0:T(128)} %scale_space.1, ...), custom_call_target="tpu_custom_call" | custom-call | flops 12000000000 | bytes 24000000 | tf_op jit(solution)/shard_map/pallas_call | solution.py:337
  73.0 0.0 copy-start
  73.1 2.4 %copy.15 = bf16[8,64,1024]{2,1,0:T(8,128)(2,1)} copy(bf16[8,64,1024]{2,1,0:T(8,128)(2,1)} %get-tuple-element.4) | data formatting | bytes 2097152
  75.4 0.0 copy-done
  75.4 1.0 %copy.16 = bf16[8,64,1024]{2,1,0:T(8,128)(2,1)} copy(bf16[8,64,1024]{2,1,0:T(8,128)(2,1)S(1)} %copy-done) | data formatting | bytes 2097152
Async XLA Ops:
  73.0 2.4 %copy-start = (bf16[8,64,1024]{2,1,0:T(8,128)(2,1)S(1)}, bf16[8,64,1024]{2,1,0:T(8,128)(2,1)}, u32[]{:S(2)}) copy-start(bf16[8,64,1024]{2,1,0:T(8,128)(2,1)} %get-tuple-element.5) | copy-start | bytes 3145732

commit v4 on v3

--- a/solution.py
+++ b/solution.py
@@ -19,13 +19,10 @@
     row = lax.broadcasted_iota(jnp.int32, (LANES, LANES), 0)
     column = lax.broadcasted_iota(jnp.int32, (LANES, LANES), 1)
     head_mean[...] = jnp.where(row // HD == column // HD, 1.0 / HD, 0.0).astype(jnp.bfloat16)
-    count = head_sum.shape[0] // heads
-    wide_column = lax.broadcasted_iota(jnp.int32, (count, LANES), 1)
     few_columns = lax.broadcasted_iota(jnp.int32, (PACK, LANES), 1)
     for h in range(heads):
-        head_sum[h * count : (h + 1) * count] = jnp.where(
-            wide_column // HD == h, 1.0, 0.0
-        ).astype(jnp.bfloat16)
+        across = (h + heads // 2) % heads
+        head_sum[h] = jnp.where(few_columns // HD == across, 1.0, 0.0).astype(jnp.bfloat16)
         head_rows[h] = jnp.where(few_columns // HD == h, 1.0, 0.0).astype(jnp.bfloat16)
     allowed[...] = jnp.where(
         (lax.rem(row, pg) == lax.rem(column, pg)) & (row >= column), 1.0, 0.0
@@ -39,7 +36,7 @@
     square = jnp.mean(x * x, -1, keepdims=True)
     normed[...] = (x * lax.rsqrt(square + 1e-05) * gain).astype(jnp.bfloat16)
     lane_head = lax.broadcasted_iota(jnp.int32, (1, LANES), 1) // HD
-    step = head_sum.shape[0] // heads
+    pair, split = heads // 2, LANES // 2
 
     def unit(part):
         mean = jnp.dot(
@@ -63,7 +60,13 @@
         query = (unit(project(0)) * (scale * (LOG2_E / HD))).astype(jnp.bfloat16)
         key = unit(project(1)).astype(jnp.bfloat16)
         value = project(2).astype(jnp.bfloat16)
-        return by_head(query), key, by_head(value)
+        values = [
+            jnp.concatenate(
+                [value * head_rows[h][:1] + head_sum[h][:1] for h in range(first, first + pair)], 0
+            )
+            for first in range(0, heads, pair)
+        ]
+        return by_head(query), key, values
 
     ready = prepare(0)
     for g in range(width // LANES):
@@ -77,16 +80,19 @@
         for h in range(heads):
             weight = jnp.exp2(scores[h * count : (h + 1) * count]).astype(jnp.bfloat16)
             weights.append(weight if allowed is None else weight * allowed[...])
-        weight = jnp.concatenate(weights, 1)
-        total = jnp.dot(weight, values, preferred_element_type=jnp.float32)
-        if step == count:
-            sums = head_sum[...]
-        else:
-            sums = jnp.concatenate(
-                [head_sum[h * step : h * step + count] for h in range(heads)], 0
+        low, high = (
+            jnp.dot(
+                jnp.concatenate(weights[first : first + pair], 1),
+                values[first // pair],
+                preferred_element_type=jnp.float32,
             )
-        denom = jnp.dot(weight, sums, preferred_element_type=jnp.float32)
-        attn[:, g * LANES : (g + 1) * LANES] = (total / denom).astype(jnp.bfloat16)
+            for first in (0, pair)
+        )
+        columns = g * LANES
+        attn[:, columns : columns + split] = (low[:, :split] / low[:, split:]).astype(jnp.bfloat16)
+        attn[:, columns + split : columns + LANES] = (high[:, split:] / high[:, :split]).astype(
+            jnp.bfloat16
+        )
     return x + jnp.dot(attn[...], out_ref[...], preferred_element_type=jnp.float32)
 
 
@@ -105,7 +111,7 @@
     scale_time,
     codebook_hbm,
     encoded,
-    commitment,
+    chosen_out,
     qkv_space,
     out_space,
     qkv_time,
@@ -200,6 +206,8 @@
             one_hot, codebook[...], preferred_element_type=jnp.float32
         ).astype(jnp.bfloat16)
 
+    keep = pltpu.make_async_copy(chosen, chosen_out, load_sem.at[5])
+    keep.start()
     loads[0].wait()
     loads[1].wait()
     for f in range(1, f_own):
@@ -228,7 +236,7 @@
         last = f == f_own - 1
 
         def send(k, carry, half):
-            other = lax.rem(me + k, n)
+            other = lax.rem(me + 1 + lax.rem(k + n_tm - 2, n - 1), n)
             to_i, to_j = lax.rem(other, n_tm), other // n_tm
             part = half if last else slice(None)
             pltpu.make_async_remote_copy(
@@ -305,10 +313,8 @@
             )
             part = pl.ds(half * (p_local // halves) + first * pg, PACK)
             encoded[:, part, :] = output.astype(jnp.bfloat16)
-            commitment[:, part, :] = (output - chosen[:, part, :].astype(jnp.float32)).astype(
-                jnp.bfloat16
-            )
-
+
+    keep.wait()
     shared(f_own - 1)
     for f in range(f_own):
         sent = packed.at[f, pl.ds(0, n_patch - 1)]
@@ -317,6 +323,13 @@
         pltpu.make_async_copy(sent, sent, mid_send).wait()
     sent = leaving.at[:, pl.ds(0, n_tm - 1)]
     pltpu.make_async_copy(sent, sent, out_send).wait()
+
+
+def finish(output, rows, encoded, commitment):
+    encoded[...] = output[...]
+    commitment[...] = (
+        output[...].astype(jnp.float32) - rows[...].astype(jnp.float32)
+    ).astype(jnp.bfloat16)
 
 
 def solution(mesh):
@@ -334,7 +347,7 @@
         vmem = pl.BlockSpec(memory_space=pltpu.VMEM)
         smem = pl.BlockSpec(memory_space=pltpu.SMEM)
         bf16, f32 = jnp.bfloat16, jnp.float32
-        return pl.pallas_call(
+        output, rows = pl.pallas_call(
             functools.partial(kernel, n_tm, n_patch),
             out_shape=[jax.ShapeDtypeStruct(x.shape, bf16)] * 2,
             in_specs=[
@@ -350,7 +363,7 @@
                 smem,
                 any_space,
             ],
-            out_specs=[vmem, vmem],
+            out_specs=[vmem, any_space],
             scratch_shapes=[
                 pltpu.VMEM(w_s.shape, bf16),
                 pltpu.VMEM(o_s.shape, bf16),
@@ -369,10 +382,10 @@
                 pltpu.VMEM((LANES, width), bf16),
                 pltpu.VMEM((LANES, width), bf16),
                 pltpu.VMEM((LANES, LANES), bf16),
-                pltpu.VMEM((LANES // HD * max(count, LANES), LANES), bf16),
+                pltpu.VMEM((LANES // HD, PACK, LANES), bf16),
                 pltpu.VMEM((LANES // HD, PACK, LANES), bf16),
                 pltpu.VMEM((LANES, LANES), bf16),
-                pltpu.SemaphoreType.DMA((5,)),
+                pltpu.SemaphoreType.DMA((6,)),
                 pltpu.SemaphoreType.DMA((f_own,)),
                 pltpu.SemaphoreType.DMA((f_own,)),
                 pltpu.SemaphoreType.DMA,
@@ -399,6 +412,15 @@
             s_t,
             book,
         )
+        block = pl.BlockSpec((max(1, f_local // 4), p_local, width), lambda f: (f, 0, 0))
+        return pl.pallas_call(
+            finish,
+            grid=(f_local // max(1, f_local // 4),),
+            out_shape=[jax.ShapeDtypeStruct(x.shape, bf16)] * 2,
+            in_specs=[block, block],
+            out_specs=[block, block],
+            compiler_params=pltpu.CompilerParams(vmem_limit_bytes=60 * 1024 * 1024),
+        )(output, rows)
 
     return jax.shard_map(
         shards,

time: 76.6 us -> 77.1 us (level)
  Pallas kernels: 72.4 us -> 76.3 us
  local copies, waits for them, and re-layouts: 3.32 us -> 0 us
    pallas_call x0 -> x1, Pallas kernels: none -> 3.73 us  [shards(): pl.pallas_call(finish, grid=(f_local // max(1, f_local // 4),), out_shape...]
    unnamed x4 -> x0, local copies, waits for them, and re-layouts: 3.32 us -> none
where the time goes in v4:
time: 77.1 us; the launch traced here: 76.9 us
  Pallas kernels  76.3 us (99%)
    pallas_call x1, Pallas kernels, shards(): pl.pallas_call(functools.partial(kernel, n_tm, n_patch), out_shape=[jax.S...  72.5 us
    pallas_call x1, Pallas kernels, shards(): pl.pallas_call(finish, grid=(f_local // max(1, f_local // 4),), out_shape...  3.73 us

profile of v4, /device:TPU:1, one launch (start us, length us, event | category | flops | bytes accessed | tf_op | source)
XLA Modules:
  0.0 76.9 jit_solution(12912457835447833324)
XLA Ops:
  0.6 72.5 %shard_map.122 = (bf16[8,64,1024]{2,1,0:T(8,128)(2,1)}, bf16[8,64,1024]{2,1,0:T(8,128)(2,1)}) custom-call(bf16[8,64,1024]{2,1,0:T(8,128)(2,1)} %x_hbm.1, s32[8,64]{1,0:T(8,128)} %codes_ref.1, f32[1,1024]{1,0:T(1,128)} %bitcast.2, bf16[1024,3072]{1,0:T(8,128)(2,1)} %qkv_space_hbm.1, bf16[1024,1024]{1,0:T(8,128)(2,1)} %out_space_hbm.1, f32[16]{0:T(128)} %scale_space.1, ...), custom_call_target="tpu_custom_call" | custom-call | flops 12000000000 | bytes 24000000 | tf_op jit(solution)/shard_map/pallas_call | solution.py:350
  73.2 3.7 %shard_map.123 = (bf16[8,64,1024]{2,1,0:T(8,128)(2,1)}, bf16[8,64,1024]{2,1,0:T(8,128)(2,1)}) custom-call(bf16[8,64,1024]{2,1,0:T(8,128)(2,1)} %get-tuple-element.4.output, bf16[8,64,1024]{2,1,0:T(8,128)(2,1)} %get-tuple-element.5.rows), custom_call_target="tpu_custom_call" | custom-call | tf_op jit(solution)/shard_map/pallas_call | solution.py:416

commit v5 on v4

--- a/solution.py
+++ b/solution.py
@@ -111,7 +111,7 @@
     scale_time,
     codebook_hbm,
     encoded,
-    chosen_out,
+    commitment,
     qkv_space,
     out_space,
     qkv_time,
@@ -206,8 +206,6 @@
             one_hot, codebook[...], preferred_element_type=jnp.float32
         ).astype(jnp.bfloat16)
 
-    keep = pltpu.make_async_copy(chosen, chosen_out, load_sem.at[5])
-    keep.start()
     loads[0].wait()
     loads[1].wait()
     for f in range(1, f_own):
@@ -236,7 +234,7 @@
         last = f == f_own - 1
 
         def send(k, carry, half):
-            other = lax.rem(me + 1 + lax.rem(k + n_tm - 2, n - 1), n)
+            other = lax.rem(me + k, n)
             to_i, to_j = lax.rem(other, n_tm), other // n_tm
             part = half if last else slice(None)
             pltpu.make_async_remote_copy(
@@ -313,8 +311,10 @@
             )
             part = pl.ds(half * (p_local // halves) + first * pg, PACK)
             encoded[:, part, :] = output.astype(jnp.bfloat16)
-
-    keep.wait()
+            commitment[:, part, :] = (output - chosen[:, part, :].astype(jnp.float32)).astype(
+                jnp.bfloat16
+            )
+
     shared(f_own - 1)
     for f in range(f_own):
         sent = packed.at[f, pl.ds(0, n_patch - 1)]
@@ -323,13 +323,6 @@
         pltpu.make_async_copy(sent, sent, mid_send).wait()
     sent = leaving.at[:, pl.ds(0, n_tm - 1)]
     pltpu.make_async_copy(sent, sent, out_send).wait()
-
-
-def finish(output, rows, encoded, commitment):
-    encoded[...] = output[...]
-    commitment[...] = (
-        output[...].astype(jnp.float32) - rows[...].astype(jnp.float32)
-    ).astype(jnp.bfloat16)
 
 
 def solution(mesh):
@@ -347,7 +340,7 @@
         vmem = pl.BlockSpec(memory_space=pltpu.VMEM)
         smem = pl.BlockSpec(memory_space=pltpu.SMEM)
         bf16, f32 = jnp.bfloat16, jnp.float32
-        output, rows = pl.pallas_call(
+        return pl.pallas_call(
             functools.partial(kernel, n_tm, n_patch),
             out_shape=[jax.ShapeDtypeStruct(x.shape, bf16)] * 2,
             in_specs=[
@@ -363,7 +356,7 @@
                 smem,
                 any_space,
             ],
-            out_specs=[vmem, any_space],
+            out_specs=[vmem, vmem],
             scratch_shapes=[
                 pltpu.VMEM(w_s.shape, bf16),
                 pltpu.VMEM(o_s.shape, bf16),
@@ -385,7 +378,7 @@
                 pltpu.VMEM((LANES // HD, PACK, LANES), bf16),
                 pltpu.VMEM((LANES // HD, PACK, LANES), bf16),
                 pltpu.VMEM((LANES, LANES), bf16),
-                pltpu.SemaphoreType.DMA((6,)),
+                pltpu.SemaphoreType.DMA((5,)),
                 pltpu.SemaphoreType.DMA((f_own,)),
                 pltpu.SemaphoreType.DMA((f_own,)),
                 pltpu.SemaphoreType.DMA,
@@ -412,15 +405,6 @@
             s_t,
             book,
         )
-        block = pl.BlockSpec((max(1, f_local // 4), p_local, width), lambda f: (f, 0, 0))
-        return pl.pallas_call(
-            finish,
-            grid=(f_local // max(1, f_local // 4),),
-            out_shape=[jax.ShapeDtypeStruct(x.shape, bf16)] * 2,
-            in_specs=[block, block],
-            out_specs=[block, block],
-            compiler_params=pltpu.CompilerParams(vmem_limit_bytes=60 * 1024 * 1024),
-        )(output, rows)
 
     return jax.shard_map(
         shards,

time: 77.1 us -> 75.4 us (0.978)
  Pallas kernels: 76.3 us -> 71.2 us
  local copies, waits for them, and re-layouts: 0 us -> 3.32 us
    pallas_call x1 -> x0, Pallas kernels: 3.73 us -> none  [shards(): pl.pallas_call(finish, grid=(f_local // max(1, f_local // 4),), out_shape...]
    unnamed x0 -> x4, local copies, waits for them, and re-layouts: none -> 3.32 us
    pallas_call x1, Pallas kernels: 72.5 us -> 71.2 us  [shards(): pl.pallas_call(functools.partial(kernel, n_tm, n_patch), out_shape=[jax.S...]
where the time goes in v5:
time: 75.4 us; the launch traced here: 75.2 us
  Pallas kernels  71.2 us (94%)
  local copies, waits for them, and re-layouts  3.32 us (4%)
    pallas_call x1, Pallas kernels, shards(): pl.pallas_call(functools.partial(kernel, n_tm, n_patch), out_shape=[jax.S...  71.2 us
    unnamed x4, local copies, waits for them, and re-layouts  3.32 us

profile of v5, /device:TPU:1, one launch (start us, length us, event | category | flops | bytes accessed | tf_op | source)
XLA Modules:
  0.0 75.2 jit_solution(5563071000605863931)
XLA Ops:
  0.6 71.2 %shard_map.122 = (bf16[8,64,1024]{2,1,0:T(8,128)(2,1)}, bf16[8,64,1024]{2,1,0:T(8,128)(2,1)}) custom-call(bf16[8,64,1024]{2,1,0:T(8,128)(2,1)} %x_hbm.1, s32[8,64]{1,0:T(8,128)} %codes_ref.1, f32[1,1024]{1,0:T(1,128)} %bitcast.2, bf16[1024,3072]{1,0:T(8,128)(2,1)} %qkv_space_hbm.1, bf16[1024,1024]{1,0:T(8,128)(2,1)} %out_space_hbm.1, f32[16]{0:T(128)} %scale_space.1, ...), custom_call_target="tpu_custom_call" | custom-call | flops 12000000000 | bytes 24000000 | tf_op jit(solution)/shard_map/pallas_call | solution.py:343
  71.9 0.0 copy-start
  71.9 2.4 %copy.15 = bf16[8,64,1024]{2,1,0:T(8,128)(2,1)} copy(bf16[8,64,1024]{2,1,0:T(8,128)(2,1)} %get-tuple-element.4) | data formatting | bytes 2097152
  74.2 0.0 copy-done
  74.2 1.0 %copy.16 = bf16[8,64,1024]{2,1,0:T(8,128)(2,1)} copy(bf16[8,64,1024]{2,1,0:T(8,128)(2,1)S(1)} %copy-done) | data formatting | bytes 2097152
Async XLA Ops:
  71.9 2.4 %copy-start = (bf16[8,64,1024]{2,1,0:T(8,128)(2,1)S(1)}, bf16[8,64,1024]{2,1,0:T(8,128)(2,1)}, u32[]{:S(2)}) copy-start(bf16[8,64,1024]{2,1,0:T(8,128)(2,1)} %get-tuple-element.5) | copy-start | bytes 3145732
